TPU v7x, 32 devices: a whole 2x2x4 slice. The times are simulated.
32 devices in a mesh: groups: 2 (over x), expert: 16 (over z, y, core).
Axes of the slice: x: 2, y: 2, z: 4, core: 2. Of those that a mesh axis runs over, the one named last changes fastest.
Arguments:
- tokens: bfloat16 [4096, 3584], P(('groups', 'expert')), parts along dimension 0, may hold values from -6 to 6
- expert_ids: int32 [4096, 8], P(('groups', 'expert')), parts along dimension 0, may hold values from 0 to 255, all different within a row
- lengths: int32 [2], P('groups'), parts along dimension 0, may hold values from 1024 to 2048
- router: bfloat16 [256, 3584], P('expert'), may hold values from -0.09375 to 0.09375
- w_gate: bfloat16 [16, 3584, 512], P('expert'), may hold values from -0.09375 to 0.09375
- w_up: bfloat16 [16, 3584, 512], P('expert'), may hold values from -0.09375 to 0.09375
- w_down: bfloat16 [16, 512, 3584], P('expert'), may hold values from -0.125 to 0.125
Outputs:
- mixed: bfloat16 [4096, 3584], P(('groups', 'expert')), parts along dimension 0
There are 2 independent parts, one for each index of `groups`. A program takes and returns all parts, laid end to end along the dimension named above; an argument that names none is the same for every part. Nothing has to cross between parts.
Inputs may be any that keep to these rules, and one draw needn't show every extreme that they name: `expert_ids`: each row names 8 different experts.
All inputs are finite; a program needn't handle non-finite values.
Results may differ from a plain program's by a relative error of at most 0.0057.
Values may be sent and summed in bfloat16 or wider, within the bound.
A program may use at most 64 MiB of HBM per device.

v0:
```python
import jax
import jax.numpy as jnp
from jax import lax
from jax.sharding import PartitionSpec as P

SPLIT = 4
SEQ_LEN = 2048
CAP = 4


def shards(tokens, expert_ids, lengths, router, w_gate, w_up, w_down):
    n_dev = lax.axis_size("expert")
    window = n_dev // SPLIT
    tok_rows = tokens.shape[0]
    routes_per = expert_ids.shape[1]
    width = tokens.shape[1]
    product = lax.dot_general(
        tokens,
        lax.all_gather(router, "expert", axis=0, tiled=True),
        (((1,), (1,)), ((), ())),
        preferred_element_type=jnp.float32,
    )
    scores = jax.nn.sigmoid(product)
    picked = jnp.take_along_axis(scores, expert_ids, axis=1)
    route_gate = 2.5 * picked / jnp.sum(picked, axis=1, keepdims=True)
    my_index = lax.axis_index("expert")
    position = my_index * tok_rows + jnp.arange(tok_rows, dtype=jnp.int32)
    sequence = position // SEQ_LEN
    seq_table = (
        sequence[:, None] == jnp.arange(lengths.shape[0], dtype=jnp.int32)[None, :]
    ).astype(jnp.int32)
    length_of = jnp.sum(seq_table * lengths[None, :], axis=1)
    is_live = position % SEQ_LEN < length_of
    flat_ids = expert_ids.reshape(tok_rows * routes_per)
    live_routes = jnp.repeat(is_live, routes_per)
    in_window = (
        (flat_ids[:, None] == jnp.arange(window, dtype=jnp.int32)[None, :]) & live_routes[:, None]
    ).astype(jnp.int32)
    slot_index = jnp.cumsum(in_window, axis=0) - in_window
    kept_route = in_window * (slot_index < CAP).astype(jnp.int32)
    slot_onehot = kept_route[..., None] * (
        slot_index[..., None] == jnp.arange(CAP, dtype=jnp.int32)
    ).astype(jnp.int32)
    slot_onehot = slot_onehot.reshape(tok_rows, routes_per, window, CAP).astype(jnp.float32)
    dispatch = jnp.sum(slot_onehot, axis=1).astype(jnp.bfloat16)
    combine = jnp.einsum("tkwc,tk->wct", slot_onehot, route_gate, precision=lax.Precision.HIGHEST)
    dispatched = jnp.einsum(
        "twc,td->wcd", dispatch, tokens, preferred_element_type=jnp.float32
    ).astype(jnp.bfloat16)
    outgoing = jnp.repeat(dispatched, SPLIT, axis=0)
    received = lax.all_to_all(outgoing, "expert", split_axis=0, concat_axis=0, tiled=True)
    sources, slots, features = received.shape
    flat_rows = received.reshape(sources * slots, features)
    gate_act = jnp.dot(flat_rows, w_gate[0], preferred_element_type=jnp.float32)
    up_act = jnp.dot(flat_rows, w_up[0], preferred_element_type=jnp.float32)
    hidden = (jax.nn.silu(gate_act) * up_act).astype(jnp.bfloat16)
    partial_value = jnp.dot(hidden, w_down[0], preferred_element_type=jnp.float32).astype(
        jnp.bfloat16
    )
    partials = partial_value.reshape(sources, slots, features)
    returned = lax.all_to_all(partials, "expert", split_axis=0, concat_axis=0, tiled=True)
    expert_out = jnp.sum(returned.reshape(window, SPLIT, CAP, width).astype(jnp.float32), axis=1)
    mixed = jnp.einsum("wct,wcd->td", combine, expert_out, precision=lax.Precision.HIGHEST)
    return mixed.astype(jnp.bfloat16)


def solution(mesh):
    placed = (
        P(("groups", "expert"), None),
        P(("groups", "expert"), None),
        P("groups"),
        P("expert", None),
        P("expert", None, None),
        P("expert", None, None),
        P("expert", None, None),
    )
    return jax.shard_map(
        shards, mesh=mesh, in_specs=placed, out_specs=P(("groups", "expert"), None), check_vma=False
    )
```

profile of v0, /device:TPU:0, one launch (start us, length us, event | category | flops | bytes accessed | tf_op | source)
XLA Modules:
  0.0 115.1 jit_solution(11822403496533072971)
XLA Ops:
  6.5 0.0 copy-start
  6.5 0.0 all-gather.2.cloned.1.call-start
  6.5 0.7 all-gather.2.cloned.1.call-update
  7.3 0.8 copy.41
  8.1 0.1 eq.53
  8.1 0.1 eq.58
  8.2 0.7 bitcast_or_fusion
  8.9 0.1 copy.39
  9.0 0.1 reshape.68
  9.8 0.1 broadcast_in_dim.22
  9.9 0.1 broadcast_in_dim.23
  10.0 1.1 reduce-window.6
  11.2 0.2 slice_reduce_fusion
  11.4 0.2 reduce-window.9
  11.6 0.1 broadcast_in_dim.24
  11.7 0.1 and.50
  11.8 0.1 add_bitcast_fusion
  11.9 0.2 mul.52
  12.0 0.1 copy.44
  12.1 0.2 eq.63
  12.3 0.1 copy.43
  12.4 40.6 %all-gather.2.cloned.1.call-done = bf16[256,3584]{1,0:T(8,128)(2,1)} async-done(((bf16[16,3584]{1,0:T(8,128)(2,1)}), bf16[256,3584]{1,0:T(8,128)(2,1)}) %all-gather.2.cloned.1.call-update) | async-done | bytes 1835024 | tf_op jit(solution)/shard_map/all_gather | solution.py:19
  53.0 0.0 copy-done
  53.0 2.2 %fusion.8 = f32[128,256]{1,0:T(8,128)S(1)} fusion(bf16[128,3584]{1,0:T(8,128)(2,1)S(1)} %copy-done, bf16[256,3584]{1,0:T(8,128)(2,1)} %all-gather.2.cloned.1.call-done), kind=kOutput, calls=%fused_computation.13 | convolution fusion | flops 234979328 | bytes 2883584 | tf_op jit(solution)/shard_map/dot_general | solution.py:17
  55.3 0.0 copy-start.1
  55.3 8.6 %gather_fusion = f32[1024]{0:T(1024)S(1)} fusion(f32[128,256]{1,0:T(8,128)S(1)} %fusion.8, s32[1024]{0:T(1024)S(1)} %reshape.68), kind=kCustom, calls=%fused_computation | custom fusion | bytes 16384 | tf_op jit(solution)/shard_map/jit(take_along_axis)/gather | solution.py:24
  63.9 0.1 reshape.71
  64.0 0.0 copy-done.1
  64.1 0.1 multiply_reduce_fusion
  64.1 0.2 convolution_convert_fusion.1
  64.4 0.1 broadcast_in_dim.25
  64.5 16.4 %all_to_all.10 = bf16[16,4,3584]{2,1,0:T(4,128)(2,1)S(1)} all-to-all(bf16[16,4,3584]{2,1,0:T(4,128)(2,1)S(1)} %bitcast.60), channel_id=1, replica_groups=mesh['groups'=2,'expert'=16] {'expert'}, dimensions={0} | all-to-all | bytes 917504 | tf_op jit(solution)/shard_map/all_to_all | solution.py:51
  80.9 0.1 reshape.65
  81.0 2.8 %fusion.4 = f32[64,512]{1,0:T(8,128)S(1)} fusion(bf16[64,3584]{1,0:T(8,128)(2,1)S(1)} %reshape.65, bf16[1,3584,512]{2,1,0:T(8,128)(2,1)} %param.11), kind=kOutput, calls=%fused_computation.8 | convolution fusion | flops 234881024 | bytes 4259840 | tf_op jit(solution)/shard_map/dot_general | solution.py:54
  83.8 4.6 %convolution_convert_fusion = bf16[64,3584]{1,0:T(8,128)(2,1)S(1)} fusion(bf16[1,512,3584]{2,1,0:T(8,128)(2,1)} %param.13, bf16[64,3584]{1,0:T(8,128)(2,1)S(1)} %reshape.65, bf16[1,3584,512]{2,1,0:T(8,128)(2,1)} %param.12, f32[64,512]{1,0:T(8,128)S(1)} %fusion.4), kind=kOutput, calls=%fused_computation.3 | convolution fusion | flops 470188032 | bytes 8388608 | tf_op jit(solution)/shard_map/dot_general | solution.py:57
  88.4 0.1 reshape.66
  88.5 16.9 %all_to_all.11 = bf16[16,4,3584]{2,1,0:T(4,128)(2,1)S(1)} all-to-all(bf16[16,4,3584]{2,1,0:T(4,128)(2,1)S(1)} %reshape.66), channel_id=1, replica_groups=mesh['groups'=2,'expert'=16] {'expert'}, dimensions={0} | all-to-all | bytes 917504 | tf_op jit(solution)/shard_map/all_to_all | solution.py:61
  105.5 0.2 convert_reduce_fusion
  105.7 2.6 %fusion = bf16[128,3584]{1,0:T(8,128)(2,1)} fusion(f32[4,4,3584]{2,1,0:T(4,128)S(1)} %convert_reduce_fusion, f32[128,4,4]{0,2,1:T(4,128)S(1)} %get-tuple-element.5), kind=kOutput, calls=%fused_computation.2 | convolution fusion | flops 88539136 | bytes 1155072 | tf_op jit(solution)/shard_map/wct,wcd->td/dot_general | solution.py:63
  (7 shorter events, 0.2 us)
Async XLA Ops:
  6.5 46.5 %copy-start = (bf16[128,3584]{1,0:T(8,128)(2,1)S(1)}, bf16[128,3584]{1,0:T(8,128)(2,1)}, u32[]{:S(2)}) copy-start(bf16[128,3584]{1,0:T(8,128)(2,1)} %param.7) | copy-start | bytes 2752516
  6.5 46.5 %all-gather.2.cloned.1.call-start = ((), (), s32[]{:S(2)}) async-start(), calls=%async_computation.2 | async-start | bytes 1949696 | tf_op jit(solution)/shard_map/all_gather | solution.py:19
  55.3 8.7 %copy-start.1 = (s32[128,8]{0,1:T(8,128)S(1)}, s32[128,8]{0,1:T(8,128)}, u32[]{:S(2)}) copy-start(s32[128,8]{0,1:T(8,128)} %param.8) | copy-start | bytes 12292
Sparse Core Ops, SparseCore 0:
  9.6 43.3 all-gather.1
where the time goes:
time: 115 us
  waiting for transfers between devices  41.3 us (36%)
  blocking collectives  33.4 us (29%)
  between operations  14.2 us (12%)
  matrix products  12.4 us (11%)
  local copies, waits for them, and re-layouts  11.3 us (10%)
  other arithmetic  2.48 us (2%)
    all_gather x1, waiting for transfers between devices, shards(): lax.all_gather(router, 'expert', axis=0, tiled=True)  40.6 us
    all_to_all x1, blocking collectives, shards(): lax.all_to_all(partials, 'expert', split_axis=0, concat_axis=0, tiled=True)  16.9 us
    all_to_all x1, blocking collectives, shards(): lax.all_to_all(outgoing, 'expert', split_axis=0, concat_axis=0, tiled=True)  16.4 us
    gather x5, local copies, waits for them, and re-layouts, shards(): picked = jnp.take_along_axis(scores, expert_ids, axis=1)  8.91 us
    dot_general x1, matrix products, shards(): jnp.dot(hidden, w_down[0], preferred_element_type=jnp.float32)  4.62 us
    dot_general x1, matrix products, shards(): gate_act = jnp.dot(flat_rows, w_gate[0], preferred_element_type=jnp.float32)  2.78 us
    dot_general x1, matrix products, shards(): jnp.einsum('wct,wcd->td', combine, expert_out, precision=lax.Precision.HI...  2.59 us
  transfers between devices with their start and end apart: 1, of which 1 were waited for; matrix products, arithmetic and copies ran while one was open for 4% of the time, Pallas kernels for 0%

commit v1 on v0

--- a/solution.py
+++ b/solution.py
@@ -14,9 +14,39 @@
     tok_rows = tokens.shape[0]
     routes_per = expert_ids.shape[1]
     width = tokens.shape[1]
+
+    def list_ports_up(arr_in, join_dim):
+        current_arr, v_now, outcome_arr = (
+            lax.axis_size("expert"),
+            lax.axis_index("expert"),
+            arr_in.shape[join_dim],
+        )
+        gallery = list(map(lambda dev: (dev, (dev + 1) % current_arr), range(current_arr)))
+        parts_seen = list(map(lambda dev: (dev, (dev - 1) % current_arr), range(current_arr)))
+        all_values = jnp.zeros(
+            (*arr_in.shape[:join_dim], current_arr * outcome_arr, *arr_in.shape[join_dim + 1 :]),
+            arr_in.dtype,
+        )
+        response = new = arr_in
+        tall = current_arr // 2
+        all_values = lax.dynamic_update_slice_in_dim(
+            all_values, arr_in, v_now * outcome_arr, axis=join_dim
+        )
+        for hop_no in range(1, tall + 1):
+            response = lax.ppermute(response, "expert", gallery)
+            all_values = lax.dynamic_update_slice_in_dim(
+                all_values, response, (v_now - hop_no) % current_arr * outcome_arr, axis=join_dim
+            )
+            if hop_no < current_arr - tall:
+                new = lax.ppermute(new, "expert", parts_seen)
+                all_values = lax.dynamic_update_slice_in_dim(
+                    all_values, new, (v_now + hop_no) % current_arr * outcome_arr, axis=join_dim
+                )
+        return all_values
+
     product = lax.dot_general(
         tokens,
-        lax.all_gather(router, "expert", axis=0, tiled=True),
+        list_ports_up(router, 0),
         (((1,), (1,)), ((), ())),
         preferred_element_type=jnp.float32,
     )

time: 115 us -> 112 us (0.974)
  starting transfers between devices: 0.01 us -> 32.2 us
  waiting for transfers between devices: 41.3 us -> 21.9 us
  between operations: 14.2 us -> 1.02 us
  matrix products: 12.4 us -> 10.9 us
  local copies, waits for them, and re-layouts: 11.3 us -> 10.1 us
    all_gather x1 -> x0, waiting for transfers between devices: 40.6 us -> none  [shards(): lax.all_gather(router, 'expert', axis=0, tiled=True)]
    ppermute x0 -> x15, starting transfers between devices: none -> 32.2 us  [the longest x7 31.7 us: list_ports_up(): new = lax.ppermute(new, 'expert', parts_seen)]
    ppermute x0 -> x15, waiting for transfers between devices: none -> 21.9 us  [the longest x8 21.9 us: list_ports_up(): response = lax.ppermute(response, 'expert', gallery)]
    dot_general x1, matrix products: 2.22 us -> 0.65 us  [shards(): lax.dot_general(tokens, list_ports_up(router, 0), (((1,), (1,)), ((), ())...]
    gather x5, local copies, waits for them, and re-layouts: 8.91 us -> 7.34 us  [shards(): picked = jnp.take_along_axis(scores, expert_ids, axis=1)]
  transfers between devices with their start and end apart: 1 -> 15, of which waited for: 1 -> 7; matrix products, arithmetic and copies ran while one was open for 4% -> 4% of each run, Pallas kernels for 0% -> 0%
where the time goes in v1:
time: 112 us; the launch traced here: 111 us
  blocking collectives  32.7 us (29%)
  starting transfers between devices  32.2 us (29%)
  waiting for transfers between devices  21.9 us (20%)
  matrix products  10.9 us (10%)
  local copies, waits for them, and re-layouts  10.1 us (9%)
  other arithmetic  2.48 us (2%)
    ppermute x7, starting transfers between devices, list_ports_up(): new = lax.ppermute(new, 'expert', parts_seen)  31.7 us
    ppermute x8, waiting for transfers between devices, list_ports_up(): response = lax.ppermute(response, 'expert', gallery)  21.9 us
    all_to_all x1, blocking collectives, shards(): lax.all_to_all(partials, 'expert', split_axis=0, concat_axis=0, tiled=True)  16.9 us
    all_to_all x1, blocking collectives, shards(): lax.all_to_all(outgoing, 'expert', split_axis=0, concat_axis=0, tiled=True)  15.9 us
    gather x5, local copies, waits for them, and re-layouts, shards(): picked = jnp.take_along_axis(scores, expert_ids, axis=1)  7.34 us
    dot_general x1, matrix products, shards(): jnp.dot(hidden, w_down[0], preferred_element_type=jnp.float32)  4.61 us
    dot_general x1, matrix products, shards(): gate_act = jnp.dot(flat_rows, w_gate[0], preferred_element_type=jnp.float32)  2.78 us
    dot_general x1, matrix products, shards(): jnp.einsum('wct,wcd->td', combine, expert_out, precision=lax.Precision.HI...  2.59 us
  transfers between devices with their start and end apart: 15, of which 7 were waited for; matrix products, arithmetic and copies ran while one was open for 4% of the time, Pallas kernels for 0%

profile of v1, /device:TPU:0, one launch (start us, length us, event | category | flops | bytes accessed | tf_op | source)
XLA Modules:
  0.0 111.3 jit_solution(7310980325021388394)
XLA Ops:
  0.0 0.5 collective-permute-start
  0.5 5.1 %collective-permute-start.1 = (bf16[16,3584]{1,0:T(8,128)(2,1)}, bf16[16,3584]{1,0:T(8,128)(2,1)S(1)}, u32[]{:S(2)}, u32[]{:S(2)}) collective-permute-start(bf16[16,3584]{1,0:T(8,128)(2,1)} %param.10), channel_id=1, source_target_pairs={{0,15},{1,0},{2,1},{3,2},{4,3},{5,4},{6,5},{7,6},{8,7},{9,8},{10,9... | collective-permute-start | bytes 344072 | tf_op jit(solution)/shard_map/ppermute | solution.py:41
  5.5 0.7 bitcast_or_fusion
  6.2 0.8 copy.41
  7.0 0.1 eq.69
  7.1 0.1 eq.74
  7.2 0.1 copy.39
  7.3 0.1 reshape.68
  8.0 0.1 broadcast_in_dim.26
  8.1 0.1 broadcast_in_dim.27
  8.3 1.1 %reduce-window.6 = s32[4,8,128]{2,1,0:T(8,128)S(1)} reduce-window(s32[4,8,128]{2,1,0:T(8,128)S(1)} %fusion.27, s32[]{:T(128)} %constant.137.clone.1), window={size=1x1x128 pad=0_0x0_0x127_0}, to_apply=%region_1.2 | reduce-window | flops 520192 | bytes 32772 | tf_op jit(solution)/shard_map/reduce-window
  9.4 0.2 slice_reduce_fusion
  9.6 0.2 reduce-window.9
  9.8 0.1 add_bitcast_fusion
  9.9 0.1 broadcast_in_dim.28
  10.0 0.1 and.126
  10.1 0.1 broadcast_in_dim.24
  10.3 0.2 eq.79
  10.4 0.1 copy.43
  10.5 0.2 mul.116
  10.7 0.1 copy.44
  10.9 0.1 collective-permute-start.2
  11.0 4.4 %collective-permute-start.3 = (bf16[16,3584]{1,0:T(8,128)(2,1)S(1)}, bf16[16,3584]{1,0:T(8,128)(2,1)S(1)}, u32[]{:S(2)}, u32[]{:S(2)}) collective-permute-start(bf16[16,3584]{1,0:T(8,128)(2,1)S(1)} %collective-permute-done.1), channel_id=1, source_target_pairs={{0,15},{1,0},{2,1},{3,2},{4,3},{5,4},{6,5},{7,6},{8,7},{9,8},{10,9... | collective-permute-start | bytes 344072 | tf_op jit(solution)/shard_map/ppermute | solution.py:41
  15.4 2.4 %collective-permute-done.2 = bf16[16,3584]{1,0:T(8,128)(2,1)S(1)} collective-permute-done((bf16[16,3584]{1,0:T(8,128)(2,1)S(1)}, bf16[16,3584]{1,0:T(8,128)(2,1)S(1)}, u32[]{:S(2)}, u32[]{:S(2)}) %collective-permute-start.2) | collective-permute-done | bytes 114720 | tf_op jit(solution)/shard_map/ppermute | solution.py:36
  17.9 4.4 %collective-permute-start.5 = (bf16[16,3584]{1,0:T(8,128)(2,1)S(1)}, bf16[16,3584]{1,0:T(8,128)(2,1)S(1)}, u32[]{:S(2)}, u32[]{:S(2)}) collective-permute-start(bf16[16,3584]{1,0:T(8,128)(2,1)S(1)} %collective-permute-done.3), channel_id=1, source_target_pairs={{0,15},{1,0},{2,1},{3,2},{4,3},{5,4},{6,5},{7,6},{8,7},{9,8},{10,9... | collective-permute-start | bytes 344072 | tf_op jit(solution)/shard_map/ppermute | solution.py:41
  22.4 2.5 %collective-permute-done.4 = bf16[16,3584]{1,0:T(8,128)(2,1)S(1)} collective-permute-done((bf16[16,3584]{1,0:T(8,128)(2,1)S(1)}, bf16[16,3584]{1,0:T(8,128)(2,1)S(1)}, u32[]{:S(2)}, u32[]{:S(2)}) %collective-permute-start.4) | collective-permute-done | bytes 114720 | tf_op jit(solution)/shard_map/ppermute | solution.py:36
  24.9 4.4 %collective-permute-start.7 = (bf16[16,3584]{1,0:T(8,128)(2,1)S(1)}, bf16[16,3584]{1,0:T(8,128)(2,1)S(1)}, u32[]{:S(2)}, u32[]{:S(2)}) collective-permute-start(bf16[16,3584]{1,0:T(8,128)(2,1)S(1)} %collective-permute-done.5), channel_id=1, source_target_pairs={{0,15},{1,0},{2,1},{3,2},{4,3},{5,4},{6,5},{7,6},{8,7},{9,8},{10,9... | collective-permute-start | bytes 344072 | tf_op jit(solution)/shard_map/ppermute | solution.py:41
  29.4 2.5 %collective-permute-done.6 = bf16[16,3584]{1,0:T(8,128)(2,1)S(1)} collective-permute-done((bf16[16,3584]{1,0:T(8,128)(2,1)S(1)}, bf16[16,3584]{1,0:T(8,128)(2,1)S(1)}, u32[]{:S(2)}, u32[]{:S(2)}) %collective-permute-start.6) | collective-permute-done | bytes 114720 | tf_op jit(solution)/shard_map/ppermute | solution.py:36
  31.9 4.4 %collective-permute-start.9 = (bf16[16,3584]{1,0:T(8,128)(2,1)S(1)}, bf16[16,3584]{1,0:T(8,128)(2,1)S(1)}, u32[]{:S(2)}, u32[]{:S(2)}) collective-permute-start(bf16[16,3584]{1,0:T(8,128)(2,1)S(1)} %collective-permute-done.7), channel_id=1, source_target_pairs={{0,15},{1,0},{2,1},{3,2},{4,3},{5,4},{6,5},{7,6},{8,7},{9,8},{10,9... | collective-permute-start | bytes 344072 | tf_op jit(solution)/shard_map/ppermute | solution.py:41
  36.4 2.5 %collective-permute-done.8 = bf16[16,3584]{1,0:T(8,128)(2,1)S(1)} collective-permute-done((bf16[16,3584]{1,0:T(8,128)(2,1)S(1)}, bf16[16,3584]{1,0:T(8,128)(2,1)S(1)}, u32[]{:S(2)}, u32[]{:S(2)}) %collective-permute-start.8) | collective-permute-done | bytes 114720 | tf_op jit(solution)/shard_map/ppermute | solution.py:36
  38.9 4.4 %collective-permute-start.11 = (bf16[16,3584]{1,0:T(8,128)(2,1)S(1)}, bf16[16,3584]{1,0:T(8,128)(2,1)S(1)}, u32[]{:S(2)}, u32[]{:S(2)}) collective-permute-start(bf16[16,3584]{1,0:T(8,128)(2,1)S(1)} %collective-permute-done.9), channel_id=1, source_target_pairs={{0,15},{1,0},{2,1},{3,2},{4,3},{5,4},{6,5},{7,6},{8,7},{9,8},{10,9... | collective-permute-start | bytes 344072 | tf_op jit(solution)/shard_map/ppermute | solution.py:41
  43.4 2.5 %collective-permute-done.10 = bf16[16,3584]{1,0:T(8,128)(2,1)S(1)} collective-permute-done((bf16[16,3584]{1,0:T(8,128)(2,1)S(1)}, bf16[16,3584]{1,0:T(8,128)(2,1)S(1)}, u32[]{:S(2)}, u32[]{:S(2)}) %collective-permute-start.10) | collective-permute-done | bytes 114720 | tf_op jit(solution)/shard_map/ppermute | solution.py:36
  46.0 4.4 %collective-permute-start.13 = (bf16[16,3584]{1,0:T(8,128)(2,1)S(1)}, bf16[16,3584]{1,0:T(8,128)(2,1)S(1)}, u32[]{:S(2)}, u32[]{:S(2)}) collective-permute-start(bf16[16,3584]{1,0:T(8,128)(2,1)S(1)} %collective-permute-done.11), channel_id=1, source_target_pairs={{0,15},{1,0},{2,1},{3,2},{4,3},{5,4},{6,5},{7,6},{8,7},{9,8},{10,9... | collective-permute-start | bytes 344072 | tf_op jit(solution)/shard_map/ppermute | solution.py:41
  50.5 2.4 %collective-permute-done.12 = bf16[16,3584]{1,0:T(8,128)(2,1)S(1)} collective-permute-done((bf16[16,3584]{1,0:T(8,128)(2,1)S(1)}, bf16[16,3584]{1,0:T(8,128)(2,1)S(1)}, u32[]{:S(2)}, u32[]{:S(2)}) %collective-permute-start.12) | collective-permute-done | bytes 114720 | tf_op jit(solution)/shard_map/ppermute | solution.py:36
  52.9 6.9 %collective-permute-done.14 = bf16[16,3584]{1,0:T(8,128)(2,1)S(1)} collective-permute-done((bf16[16,3584]{1,0:T(8,128)(2,1)S(1)}, bf16[16,3584]{1,0:T(8,128)(2,1)S(1)}, u32[]{:S(2)}, u32[]{:S(2)}) %collective-permute-start.14) | collective-permute-done | bytes 114720 | tf_op jit(solution)/shard_map/ppermute | solution.py:36
  59.8 0.6 fusion.9
  60.5 7.0 %gather_fusion = f32[1024]{0:T(1024)S(1)} fusion(f32[128,256]{0,1:T(8,128)S(1)} %fusion.9, s32[1024]{0:T(1024)S(1)} %reshape.68), kind=kCustom, calls=%fused_computation | custom fusion | bytes 16384 | tf_op jit(solution)/shard_map/jit(take_along_axis)/gather | solution.py:54
  67.5 0.1 reshape.71
  67.8 0.2 convolution_convert_fusion.1
  68.0 0.1 broadcast_in_dim.29
  68.1 15.9 %all_to_all.10 = bf16[16,4,3584]{2,1,0:T(4,128)(2,1)S(1)} all-to-all(bf16[16,4,3584]{2,1,0:T(4,128)(2,1)S(1)} %bitcast.62), channel_id=1, replica_groups=mesh['groups'=2,'expert'=16] {'expert'}, dimensions={0} | all-to-all | bytes 917504 | tf_op jit(solution)/shard_map/all_to_all | solution.py:81
  84.0 0.1 reshape.65
  84.1 2.8 %fusion.4 = f32[64,512]{1,0:T(8,128)S(1)} fusion(bf16[64,3584]{1,0:T(8,128)(2,1)S(1)} %reshape.65, bf16[1,3584,512]{2,1,0:T(8,128)(2,1)} %param.11), kind=kOutput, calls=%fused_computation.8 | convolution fusion | flops 234881024 | bytes 4259840 | tf_op jit(solution)/shard_map/dot_general | solution.py:84
  86.9 4.6 %convolution_convert_fusion = bf16[64,3584]{1,0:T(8,128)(2,1)S(1)} fusion(bf16[1,512,3584]{2,1,0:T(8,128)(2,1)} %param.13, bf16[64,3584]{1,0:T(8,128)(2,1)S(1)} %reshape.65, bf16[1,3584,512]{2,1,0:T(8,128)(2,1)} %param.12, f32[64,512]{1,0:T(8,128)S(1)} %fusion.4), kind=kOutput, calls=%fused_computation.3 | convolution fusion | flops 470188032 | bytes 8388608 | tf_op jit(solution)/shard_map/dot_general | solution.py:87
  91.5 0.1 reshape.66
  91.6 16.9 %all_to_all.11 = bf16[16,4,3584]{2,1,0:T(4,128)(2,1)S(1)} all-to-all(bf16[16,4,3584]{2,1,0:T(4,128)(2,1)S(1)} %reshape.66), channel_id=1, replica_groups=mesh['groups'=2,'expert'=16] {'expert'}, dimensions={0} | all-to-all | bytes 917504 | tf_op jit(solution)/shard_map/all_to_all | solution.py:91
  108.5 0.2 convert_reduce_fusion
  108.7 2.6 %fusion = bf16[128,3584]{1,0:T(8,128)(2,1)} fusion(f32[4,4,3584]{2,1,0:T(4,128)S(1)} %convert_reduce_fusion, f32[128,4,4]{0,2,1:T(4,128)S(1)} %get-tuple-element.5), kind=kOutput, calls=%fused_computation.2 | convolution fusion | flops 88539136 | bytes 1155072 | tf_op jit(solution)/shard_map/wct,wcd->td/dot_general | solution.py:93
  (44 shorter events, 0.5 us)
Async XLA Ops:
  0.0 59.8 %copy-start = (bf16[128,3584]{1,0:T(8,128)(2,1)S(1)}, bf16[128,3584]{1,0:T(8,128)(2,1)}, u32[]{:S(2)}) copy-start(bf16[128,3584]{1,0:T(8,128)(2,1)} %param.7) | copy-start | bytes 2752516
  0.0 10.2 %copy-start.1 = (bf16[16,3584]{1,0:T(8,128)(2,1)S(1)}, bf16[16,3584]{1,0:T(8,128)(2,1)}, u32[]{:S(2)}) copy-start(bf16[16,3584]{1,0:T(8,128)(2,1)} %param.10) | copy-start | bytes 344068
  0.0 10.9 %collective-permute-start = (bf16[16,3584]{1,0:T(8,128)(2,1)}, bf16[16,3584]{1,0:T(8,128)(2,1)S(1)}, u32[]{:S(2)}, u32[]{:S(2)}) collective-permute-start(bf16[16,3584]{1,0:T(8,128)(2,1)} %param.10), channel_id=1, source_target_pairs={{0,1},{1,2},{2,3},{3,4},{4,5},{5,6},{6,7},{7,8},{8,9},{9,10},{10,1... | collective-permute-start | bytes 344072 | tf_op jit(solution)/shard_map/ppermute | solution.py:36
  0.5 10.5 %collective-permute-start.1 = (bf16[16,3584]{1,0:T(8,128)(2,1)}, bf16[16,3584]{1,0:T(8,128)(2,1)S(1)}, u32[]{:S(2)}, u32[]{:S(2)}) collective-permute-start(bf16[16,3584]{1,0:T(8,128)(2,1)} %param.10), channel_id=1, source_target_pairs={{0,15},{1,0},{2,1},{3,2},{4,3},{5,4},{6,5},{7,6},{8,7},{9,8},{10,9... | collective-permute-start | bytes 344072 | tf_op jit(solution)/shard_map/ppermute | solution.py:41
  10.9 7.0 %collective-permute-start.2 = (bf16[16,3584]{1,0:T(8,128)(2,1)S(1)}, bf16[16,3584]{1,0:T(8,128)(2,1)S(1)}, u32[]{:S(2)}, u32[]{:S(2)}) collective-permute-start(bf16[16,3584]{1,0:T(8,128)(2,1)S(1)} %collective-permute-done), channel_id=1, source_target_pairs={{0,1},{1,2},{2,3},{3,4},{4,5},{5,6},{6,7},{7,8},{8,9},{9,10},{10,1... | collective-permute-start | bytes 344072 | tf_op jit(solution)/shard_map/ppermute | solution.py:36
  11.0 6.9 %collective-permute-start.3 = (bf16[16,3584]{1,0:T(8,128)(2,1)S(1)}, bf16[16,3584]{1,0:T(8,128)(2,1)S(1)}, u32[]{:S(2)}, u32[]{:S(2)}) collective-permute-start(bf16[16,3584]{1,0:T(8,128)(2,1)S(1)} %collective-permute-done.1), channel_id=1, source_target_pairs={{0,15},{1,0},{2,1},{3,2},{4,3},{5,4},{6,5},{7,6},{8,7},{9,8},{10,9... | collective-permute-start | bytes 344072 | tf_op jit(solution)/shard_map/ppermute | solution.py:41
  17.9 7.0 %collective-permute-start.4 = (bf16[16,3584]{1,0:T(8,128)(2,1)S(1)}, bf16[16,3584]{1,0:T(8,128)(2,1)S(1)}, u32[]{:S(2)}, u32[]{:S(2)}) collective-permute-start(bf16[16,3584]{1,0:T(8,128)(2,1)S(1)} %collective-permute-done.2), channel_id=1, source_target_pairs={{0,1},{1,2},{2,3},{3,4},{4,5},{5,6},{6,7},{7,8},{8,9},{9,10},{10,1... | collective-permute-start | bytes 344072 | tf_op jit(solution)/shard_map/ppermute | solution.py:36
  17.9 7.0 %collective-permute-start.5 = (bf16[16,3584]{1,0:T(8,128)(2,1)S(1)}, bf16[16,3584]{1,0:T(8,128)(2,1)S(1)}, u32[]{:S(2)}, u32[]{:S(2)}) collective-permute-start(bf16[16,3584]{1,0:T(8,128)(2,1)S(1)} %collective-permute-done.3), channel_id=1, source_target_pairs={{0,15},{1,0},{2,1},{3,2},{4,3},{5,4},{6,5},{7,6},{8,7},{9,8},{10,9... | collective-permute-start | bytes 344072 | tf_op jit(solution)/shard_map/ppermute | solution.py:41
  24.9 7.0 %collective-permute-start.6 = (bf16[16,3584]{1,0:T(8,128)(2,1)S(1)}, bf16[16,3584]{1,0:T(8,128)(2,1)S(1)}, u32[]{:S(2)}, u32[]{:S(2)}) collective-permute-start(bf16[16,3584]{1,0:T(8,128)(2,1)S(1)} %collective-permute-done.4), channel_id=1, source_target_pairs={{0,1},{1,2},{2,3},{3,4},{4,5},{5,6},{6,7},{7,8},{8,9},{9,10},{10,1... | collective-permute-start | bytes 344072 | tf_op jit(solution)/shard_map/ppermute | solution.py:36
  24.9 7.0 %collective-permute-start.7 = (bf16[16,3584]{1,0:T(8,128)(2,1)S(1)}, bf16[16,3584]{1,0:T(8,128)(2,1)S(1)}, u32[]{:S(2)}, u32[]{:S(2)}) collective-permute-start(bf16[16,3584]{1,0:T(8,128)(2,1)S(1)} %collective-permute-done.5), channel_id=1, source_target_pairs={{0,15},{1,0},{2,1},{3,2},{4,3},{5,4},{6,5},{7,6},{8,7},{9,8},{10,9... | collective-permute-start | bytes 344072 | tf_op jit(solution)/shard_map/ppermute | solution.py:41
  31.9 7.0 %collective-permute-start.8 = (bf16[16,3584]{1,0:T(8,128)(2,1)S(1)}, bf16[16,3584]{1,0:T(8,128)(2,1)S(1)}, u32[]{:S(2)}, u32[]{:S(2)}) collective-permute-start(bf16[16,3584]{1,0:T(8,128)(2,1)S(1)} %collective-permute-done.6), channel_id=1, source_target_pairs={{0,1},{1,2},{2,3},{3,4},{4,5},{5,6},{6,7},{7,8},{8,9},{9,10},{10,1... | collective-permute-start | bytes 344072 | tf_op jit(solution)/shard_map/ppermute | solution.py:36
  31.9 7.0 %collective-permute-start.9 = (bf16[16,3584]{1,0:T(8,128)(2,1)S(1)}, bf16[16,3584]{1,0:T(8,128)(2,1)S(1)}, u32[]{:S(2)}, u32[]{:S(2)}) collective-permute-start(bf16[16,3584]{1,0:T(8,128)(2,1)S(1)} %collective-permute-done.7), channel_id=1, source_target_pairs={{0,15},{1,0},{2,1},{3,2},{4,3},{5,4},{6,5},{7,6},{8,7},{9,8},{10,9... | collective-permute-start | bytes 344072 | tf_op jit(solution)/shard_map/ppermute | solution.py:41
  38.9 7.0 %collective-permute-start.10 = (bf16[16,3584]{1,0:T(8,128)(2,1)S(1)}, bf16[16,3584]{1,0:T(8,128)(2,1)S(1)}, u32[]{:S(2)}, u32[]{:S(2)}) collective-permute-start(bf16[16,3584]{1,0:T(8,128)(2,1)S(1)} %collective-permute-done.8), channel_id=1, source_target_pairs={{0,1},{1,2},{2,3},{3,4},{4,5},{5,6},{6,7},{7,8},{8,9},{9,10},{10,1... | collective-permute-start | bytes 344072 | tf_op jit(solution)/shard_map/ppermute | solution.py:36
  38.9 7.0 %collective-permute-start.11 = (bf16[16,3584]{1,0:T(8,128)(2,1)S(1)}, bf16[16,3584]{1,0:T(8,128)(2,1)S(1)}, u32[]{:S(2)}, u32[]{:S(2)}) collective-permute-start(bf16[16,3584]{1,0:T(8,128)(2,1)S(1)} %collective-permute-done.9), channel_id=1, source_target_pairs={{0,15},{1,0},{2,1},{3,2},{4,3},{5,4},{6,5},{7,6},{8,7},{9,8},{10,9... | collective-permute-start | bytes 344072 | tf_op jit(solution)/shard_map/ppermute | solution.py:41
  46.0 6.9 %collective-permute-start.12 = (bf16[16,3584]{1,0:T(8,128)(2,1)S(1)}, bf16[16,3584]{1,0:T(8,128)(2,1)S(1)}, u32[]{:S(2)}, u32[]{:S(2)}) collective-permute-start(bf16[16,3584]{1,0:T(8,128)(2,1)S(1)} %collective-permute-done.10), channel_id=1, source_target_pairs={{0,1},{1,2},{2,3},{3,4},{4,5},{5,6},{6,7},{7,8},{8,9},{9,10},{10,1... | collective-permute-start | bytes 344072 | tf_op jit(solution)/shard_map/ppermute | solution.py:36
  46.0 6.9 %collective-permute-start.13 = (bf16[16,3584]{1,0:T(8,128)(2,1)S(1)}, bf16[16,3584]{1,0:T(8,128)(2,1)S(1)}, u32[]{:S(2)}, u32[]{:S(2)}) collective-permute-start(bf16[16,3584]{1,0:T(8,128)(2,1)S(1)} %collective-permute-done.11), channel_id=1, source_target_pairs={{0,15},{1,0},{2,1},{3,2},{4,3},{5,4},{6,5},{7,6},{8,7},{9,8},{10,9... | collective-permute-start | bytes 344072 | tf_op jit(solution)/shard_map/ppermute | solution.py:41
  52.9 6.9 %collective-permute-start.14 = (bf16[16,3584]{1,0:T(8,128)(2,1)S(1)}, bf16[16,3584]{1,0:T(8,128)(2,1)S(1)}, u32[]{:S(2)}, u32[]{:S(2)}) collective-permute-start(bf16[16,3584]{1,0:T(8,128)(2,1)S(1)} %collective-permute-done.12), channel_id=1, source_target_pairs={{0,1},{1,2},{2,3},{3,4},{4,5},{5,6},{6,7},{7,8},{8,9},{9,10},{10,1... | collective-permute-start | bytes 344072 | tf_op jit(solution)/shard_map/ppermute | solution.py:36
  60.5 7.2 %copy-start.2 = (s32[128,8]{0,1:T(8,128)S(1)}, s32[128,8]{0,1:T(8,128)}, u32[]{:S(2)}) copy-start(s32[128,8]{0,1:T(8,128)} %param.8) | copy-start | bytes 12292
